TPU v7x, 32 devices: a whole 2x2x4 slice. The times are simulated.
32 devices in a mesh: dp: 4 (over y, x), vocab: 8 (over z, core).
Axes of the slice: x: 2, y: 2, z: 4, core: 2. Of those that a mesh axis runs over, the one named last changes fastest.
Arguments:
- hidden: bfloat16 [128, 3584], P(('dp', 'vocab')), may hold values from -6 to 6
- head_weight: bfloat16 [3584, 256000], P(None, ('dp', 'vocab')), may hold values from -0.75 to 0.75
- teacher_ids: int32 [128, 128], P(('dp', 'vocab')), may hold values from 0 to 255999
- teacher_probs: float32 [128, 128], P(('dp', 'vocab')), may hold values from 0.0001 to 0.015
- target_ids: int32 [128], P(('dp', 'vocab')), may hold values from 0 to 255999
Outputs:
- token_loss: float32 [128], P(('dp', 'vocab'))
- hidden_grad: bfloat16 [128, 3584], P(('dp', 'vocab'))
All inputs are finite; a program needn't handle non-finite values.
Results may differ from a plain program's by a relative error of at most 0.004.
Values may be sent and summed in bfloat16 or wider, within the bound.
A program may use at most 128 MiB of HBM per device.

v0:
```python
import jax
import jax.numpy as jnp
from jax import lax
from jax.sharding import PartitionSpec as P

SOFT_CAP = 30.0
CE_WEIGHT = 0.5
LOSS_SCALE = 8.0
BLOCK_ROWS = 32


def sparse_rows(teacher_ids, teacher_probs, columns):
    token_count, kept = teacher_ids.shape
    block_rows = BLOCK_ROWS
    id_blocks = teacher_ids.reshape(token_count // block_rows, block_rows, kept)
    prob_blocks = teacher_probs.reshape(token_count // block_rows, block_rows, kept)

    def one_block(pair):
        id_rows, prob_rows = pair
        match = id_rows[:, :, None] == columns[None, None, :]
        return jnp.sum(jnp.where(match, prob_rows[:, :, None], 0.0), axis=1)

    summed = lax.map(one_block, (id_blocks, prob_blocks))
    return summed.reshape(token_count, columns.shape[0])


def per_device(hidden, head_weight, teacher_ids, teacher_probs, target_ids):
    slice_width = head_weight.shape[1]
    tokens_local = hidden.shape[0]
    position = lax.axis_index(("dp", "vocab"))
    first_column = position * slice_width
    columns = first_column + jnp.arange(slice_width, dtype=jnp.int32)
    raw_logits = jnp.dot(
        lax.all_gather(hidden, ("dp", "vocab"), axis=0, tiled=True),
        head_weight,
        preferred_element_type=jnp.float32,
    )
    capped = SOFT_CAP * jnp.tanh(raw_logits / SOFT_CAP)
    all_ids, all_targets = (
        lax.all_gather(teacher_ids, ("dp", "vocab"), axis=0, tiled=True),
        lax.all_gather(target_ids, ("dp", "vocab"), axis=0, tiled=True),
    )
    all_probs = lax.all_gather(teacher_probs, ("dp", "vocab"), axis=0, tiled=True)
    sparse = sparse_rows(all_ids, all_probs, columns)
    target_hit = columns[None, :] == all_targets[:, None]
    part_dot = jnp.sum(capped * sparse, axis=1)
    part_target = jnp.sum(jnp.where(target_hit, capped, 0.0), axis=1)
    part_exp = jnp.sum(jnp.exp(capped), axis=1)
    exp_sum, teacher_dot, target_logit = lax.psum(
        (part_exp, part_dot, part_target), ("dp", "vocab")
    )
    log_total = jnp.log(exp_sum)
    teacher_sum = jnp.sum(all_probs, axis=1)
    every_loss = (
        jnp.sum(all_probs * jnp.log(all_probs), axis=1)
        - teacher_dot
        + teacher_sum * log_total
        + CE_WEIGHT * (log_total - target_logit)
    )
    token_loss = lax.dynamic_slice_in_dim(every_loss, position * tokens_local, tokens_local)
    softmax_rows = jnp.exp(capped - log_total[:, None])
    onehot = jnp.where(target_hit, 1.0, 0.0)
    raw_grads = LOSS_SCALE * (
        (teacher_sum + CE_WEIGHT)[:, None] * softmax_rows - sparse - CE_WEIGHT * onehot
    )
    grads = (raw_grads * (1.0 - (capped / SOFT_CAP) ** 2)).astype(jnp.bfloat16)
    summed = lax.psum_scatter(
        jnp.einsum("tv,dv->td", grads, head_weight, preferred_element_type=jnp.float32),
        ("dp", "vocab"),
        scatter_dimension=0,
        tiled=True,
    )
    return (token_loss, summed.astype(jnp.bfloat16))


def solution(mesh):
    in_specs = (
        P(("dp", "vocab"), None),
        P(None, ("dp", "vocab")),
        P(("dp", "vocab"), None),
        P(("dp", "vocab"), None),
        P(("dp", "vocab")),
    )
    out_specs = (P(("dp", "vocab")), P(("dp", "vocab"), None))
    return jax.shard_map(
        per_device, mesh=mesh, in_specs=in_specs, out_specs=out_specs, check_vma=False
    )
```

profile of v0, /device:TPU:1, one launch (start us, length us, event | category | flops | bytes accessed | tf_op | source)
XLA Modules:
  0.0 489.2 jit_solution(7940874425076551939)
XLA Ops:
  0.6 0.9 dynamic-update-slice
  1.5 40.6 %all-reduce = s32[128]{0:T(128)S(1)} all-reduce(s32[128]{0:T(128)S(1)} %dynamic-update-slice), channel_id=1, replica_groups=mesh['dp'=4,'vocab'=8] {'dp','vocab'}, use_global_device_ids=true, to_apply=%add | all-reduce | flops 128 | bytes 1024
  42.1 42.0 %all-gather.2 = s32[32,4,128]{2,1,0:T(4,128)S(1)} all-gather(s32[1,4,128]{2,1,0:T(4,128)} %bitcast.28), channel_id=1, replica_groups=mesh['dp'=4,'vocab'=8] {'dp','vocab'}, dimensions={0}, use_global_device_ids=true | all-gather | bytes 67584 | tf_op jit(solution)/shard_map/all_gather | solution.py:40
  84.0 37.1 %all-gather = f32[32,4,128]{2,1,0:T(4,128)S(1)} all-gather(f32[1,4,128]{2,1,0:T(4,128)} %bitcast.29), channel_id=1, replica_groups=mesh['dp'=4,'vocab'=8] {'dp','vocab'}, dimensions={0}, use_global_device_ids=true | all-gather | bytes 67584 | tf_op jit(solution)/shard_map/all_gather | solution.py:43
  121.1 171.5 %while.11 = (s32[]{:T(128)}, f32[4,32,8000]{2,1,0:T(8,128)}, s32[4,32,128]{2,1,0:T(8,128)S(1)}, f32[4,32,128]{2,1,0:T(8,128)S(1)}, s32[]{:T(128)}, /*index=5*/s32[]{:T(128)}) while((s32[]{:T(128)}, f32[4,32,8000]{2,1,0:T(8,128)}, s32[4,32,128]{2,1,0:T(8,128)S(1)}, f32[4,32,128]{2,1,0:T(8,128)S(1)}, s32[]{:T(128)}, ...), condition=%wide.region_3.4_spmd.clone, body=%wide.region_1.3_spmd.clone.sunk | while | flops 98056000 | bytes 3242589 | solution.py:23
  121.2 41.8 %select_reduce_fusion.2 = f32[32,8000]{1,0:T(8,128)S(1)} fusion(f32[32,128]{1,0:T(8,128)S(1)} %dynamic-slice_bitcast_fusion.4, s32[32,128]{1,0:T(8,128)S(1)} %dynamic-slice_bitcast_fusion.5, s32[8000]{0:T(1024)S(1)} %iota_add_fusion.3), kind=kLoop, calls=%fused_computation.1.clone.1 | loop fusion | flops 98048000 | bytes 1088768 | tf_op jit(solution)/shard_map/while/body/eval_jaxpr/reduce_sum | solution.py:21
  162.9 1.1 bitcast_dynamic-update-slice_fusion.2
  164.0 41.8 %select_reduce_fusion.2 = f32[32,8000]{1,0:T(8,128)S(1)} fusion(f32[32,128]{1,0:T(8,128)S(1)} %dynamic-slice_bitcast_fusion.4, s32[32,128]{1,0:T(8,128)S(1)} %dynamic-slice_bitcast_fusion.5, s32[8000]{0:T(1024)S(1)} %iota_add_fusion.3), kind=kLoop, calls=%fused_computation.1.clone.1 | loop fusion | flops 98048000 | bytes 1088768 | tf_op jit(solution)/shard_map/while/body/eval_jaxpr/reduce_sum | solution.py:21
  205.8 1.1 bitcast_dynamic-update-slice_fusion.2
  206.9 41.8 %select_reduce_fusion.2 = f32[32,8000]{1,0:T(8,128)S(1)} fusion(f32[32,128]{1,0:T(8,128)S(1)} %dynamic-slice_bitcast_fusion.4, s32[32,128]{1,0:T(8,128)S(1)} %dynamic-slice_bitcast_fusion.5, s32[8000]{0:T(1024)S(1)} %iota_add_fusion.3), kind=kLoop, calls=%fused_computation.1.clone.1 | loop fusion | flops 98048000 | bytes 1088768 | tf_op jit(solution)/shard_map/while/body/eval_jaxpr/reduce_sum | solution.py:21
  248.7 1.0 bitcast_dynamic-update-slice_fusion.2
  249.8 41.8 %select_reduce_fusion.2 = f32[32,8000]{1,0:T(8,128)S(1)} fusion(f32[32,128]{1,0:T(8,128)S(1)} %dynamic-slice_bitcast_fusion.4, s32[32,128]{1,0:T(8,128)S(1)} %dynamic-slice_bitcast_fusion.5, s32[8000]{0:T(1024)S(1)} %iota_add_fusion.3), kind=kLoop, calls=%fused_computation.1.clone.1 | loop fusion | flops 98048000 | bytes 1088768 | tf_op jit(solution)/shard_map/while/body/eval_jaxpr/reduce_sum | solution.py:21
  291.6 1.0 bitcast_dynamic-update-slice_fusion.2
  292.6 5.6 %copy.12 = f32[128,8000]{0,1:T(8,128)} copy(f32[128,8000]{1,0:T(8,128)} %bitcast.22) | data formatting | bytes 8192000 | tf_op jit(solution)/shard_map/reshape | solution.py:24
  298.3 41.8 %all-gather.1 = bf16[32,4,3584]{2,1,0:T(4,128)(2,1)S(1)} all-gather(bf16[1,4,3584]{2,1,0:T(4,128)(2,1)S(1)} %bitcast.27), channel_id=1, replica_groups=mesh['dp'=4,'vocab'=8] {'dp','vocab'}, dimensions={0}, use_global_device_ids=true | all-gather | bytes 946176 | tf_op jit(solution)/shard_map/all_gather | solution.py:34
  340.1 0.2 reshape.35
  340.3 25.1 %exponential_reduce_fusion = (f32[128]{0:T(128)S(1)}, f32[128]{0:T(128)S(1)}, f32[128]{0:T(128)S(1)}, f32[128,8000]{0,1:T(8,128)}) fusion(s32[128]{0:T(128)S(1)} %all-reduce, s32[8000]{0:T(1024)S(1)} %iota_add_fusion.1, f32[128,8000]{0,1:T(8,128)} %copy.12, bf16[128,3584]{1,0:T(8,128)(2,1)S(1)} %reshape.35, bf16[3584,8000]{0,1:T(8,128)(2,1)} %param.8), kind=kOutput, calls=%fused_computation.16 | convolution fusion | flops 7348224000 | bytes 66487552 | tf_op jit(solution)/shard_map/dot_general | solution.py:33
  365.5 36.5 %psum.22 = f32[128]{0:T(128)S(1)} all-reduce(f32[128]{0:T(128)S(1)} %get-tuple-element.43), channel_id=1, replica_groups=mesh['dp'=4,'vocab'=8] {'dp','vocab'}, use_global_device_ids=true, to_apply=%region_8.9 | all-reduce | flops 128 | bytes 1024 | tf_op jit(solution)/shard_map/psum | solution.py:49
  402.0 0.1 reduce
  402.2 23.4 %fusion.9 = f32[128,3584]{1,0:T(8,128)S(1)} fusion(bf16[3584,8000]{0,1:T(8,128)(2,1)} %param.8, f32[128,8000]{0,1:T(8,128)} %get-tuple-element.59, f32[128,8000]{0,1:T(8,128)} %copy.12, f32[128]{0:T(128)S(1)} %log.7, f32[128]{0:T(128)S(1)} %broadcast_add_fusion, s32[128]{0:T(128)S(1)} %all-reduce, s32[8000]{0:T(1024)S(1)} %iota_add_fusion.1), kind=kOutput, calls=%fused_computation.18 | convolution fusion | flops 7353344000 | bytes 67404544 | tf_op jit(solution)/shard_map/tv,dv->td/dot_general | solution.py:68
  425.6 62.2 %all-reduce.4 = (f32[128]{0:T(128)S(1)}, f32[128]{0:T(128)S(1)}, bf16[128,3584]{1,0:T(8,128)(2,1)S(1)}) all-reduce(f32[128]{0:T(128)S(1)} %get-tuple-element.44, f32[128]{0:T(128)S(1)} %get-tuple-element.45, f32[128,3584]{1,0:T(8,128)S(1)} %fusion.9), channel_id=1, replica_groups=mesh['dp'=4,'vocab'=8] {'dp','vocab'}, use_global_device_ids=true, to_apply=%region_10.11 | all-reduce | flops 459008 | bytes 2754560 | tf_op jit(solution)/shard_map/psum | solution.py:49
  487.9 0.1 fusion.20
  488.0 0.6 dynamic_slice.11
  488.6 0.6 dynamic-slice_convert_fusion
  (21 shorter events, 0.2 us)
Async XLA Ops:
  292.6 5.6 %copy-start = (bf16[4,3584]{1,0:T(4,128)(2,1)S(1)}, bf16[4,3584]{1,0:T(4,128)(2,1)}, u32[]{:S(2)}) copy-start(bf16[4,3584]{1,0:T(4,128)(2,1)} %param.7) | copy-start | bytes 86020
where the time goes:
time: 492 us; the launch traced here: 489 us
  blocking collectives  260 us (53%)
  other arithmetic  167 us (34%)
  matrix products  48.5 us (10%)
  local copies, waits for them, and re-layouts  12.3 us (2%)
    reduce_sum x4, other arithmetic, one_block(): return jnp.sum(jnp.where(match, prob_rows[:, :, None], 0.0), axis=1)  167 us
    psum x2, blocking collectives, per_device(): lax.psum((part_exp, part_dot, part_target), ('dp', 'vocab'))  98.8 us
    all_gather x1, blocking collectives, per_device(): lax.all_gather(teacher_ids, ('dp', 'vocab'), axis=0, tiled=True)  42 us
    all_gather x1, blocking collectives, per_device(): lax.all_gather(hidden, ('dp', 'vocab'), axis=0, tiled=True)  41.8 us
    unnamed x1, blocking collectives  40.6 us
    all_gather x1, blocking collectives, per_device(): lax.all_gather(teacher_probs, ('dp', 'vocab'), axis=0, tiled=True)  37.1 us
    dot_general x1, matrix products, per_device(): jnp.dot(lax.all_gather(hidden, ('dp', 'vocab'), axis=0, tiled=True), head...  25.1 us
    dot_general x1, matrix products, per_device(): jnp.einsum('tv,dv->td', grads, head_weight, preferred_element_type=jnp.fl...  23.4 us

commit v1 on v0

v1 whole, which is shorter than its diff:
```python
import functools
import jax
import jax.numpy as jnp
from jax import lax
from jax.experimental import pallas as pl
from jax.experimental.pallas import tpu as pltpu
from jax.sharding import PartitionSpec as P

SOFT_CAP = 30.0
CE_WEIGHT = 0.5
LOSS_SCALE = 8.0
BLOCK = 512
LANES = 128
ROW_CHUNK = 512
AXES = ("dp", "vocab")
NT = (((1,), (1,)), ((), ()))


def head_kernel(width, hidden_ref, w_ref, ids_ref, hi_probs_ref, lo_probs_ref, targets_ref,
                acc_ref, stats_ref, sparse_ref):
    step = pl.program_id(0)
    steps = pl.num_programs(0)
    tokens, depth = hidden_ref.shape
    kept = ids_ref.shape[1]
    groups = sparse_ref.shape[0]
    group_rows = 16 * pl.cdiv(groups, 16)

    @pl.when(step == 0)
    def _():
        acc_ref[...] = jnp.zeros_like(acc_ref)
        stats_ref[...] = jnp.zeros_like(stats_ref)
        group_row = lax.broadcasted_iota(jnp.int32, (group_rows, kept), 0)
        lane_row = lax.broadcasted_iota(jnp.int32, (LANES, kept), 0)

        def one_token(t, carry):
            ids = ids_ref[pl.ds(t, 1), :]
            high = jnp.where(group_row == (ids >> 7), 1.0, 0.0).astype(jnp.bfloat16)
            same = lane_row == (ids & 127)
            first = jnp.where(same, hi_probs_ref[pl.ds(t, 1), :], 0.0).astype(jnp.bfloat16)
            second = jnp.where(same, lo_probs_ref[pl.ds(t, 1), :], 0.0).astype(jnp.bfloat16)
            rows = lax.dot_general(
                jnp.concatenate([high, high], axis=1),
                jnp.concatenate([first, second], axis=1),
                NT, preferred_element_type=jnp.float32)
            sparse_ref[:, pl.ds(t, 1), :] = rows[:groups].reshape(groups, 1, LANES)
            return carry

        lax.fori_loop(0, tokens, one_token, 0, unroll=8)

    def block(columns, valid, w):
        logits = jnp.dot(hidden_ref[...], w(0, depth), preferred_element_type=jnp.float32)
        ratio = jnp.tanh(logits * (1.0 / SOFT_CAP))
        capped = SOFT_CAP * ratio
        slope = 1.0 - ratio * ratio
        lane = lax.broadcasted_iota(jnp.int32, (tokens, columns), 1)
        exps = jnp.exp(capped)
        sparse = jnp.concatenate(
            [sparse_ref[step * (BLOCK // LANES) + i] for i in range(columns // LANES)], axis=1)
        sparse = sparse + jnp.where(lane + step * BLOCK == targets_ref[...], CE_WEIGHT, 0.0)
        if valid != columns:
            inside = lane < valid
            exps = jnp.where(inside, exps, 0.0)
            sparse = jnp.where(inside, sparse, 0.0)
        stats_ref[:, 0:1] += jnp.sum(exps, axis=1, keepdims=True)
        stats_ref[:, 1:2] += jnp.sum(capped * sparse, axis=1, keepdims=True)
        grads = jnp.concatenate([exps * slope, sparse * slope], axis=0).astype(jnp.bfloat16)

        def chunk(i, carry):
            rows = pl.ds(pl.multiple_of(i * ROW_CHUNK, ROW_CHUNK), ROW_CHUNK)
            acc_ref[:, rows] += lax.dot_general(
                grads, w(i * ROW_CHUNK, ROW_CHUNK), NT, preferred_element_type=jnp.float32)
            return carry

        for i in range(depth // ROW_CHUNK):
            chunk(i, 0)

    last = width - (pl.cdiv(width, BLOCK) - 1) * BLOCK
    last_columns = LANES * pl.cdiv(last, LANES)

    @pl.when(step < steps - 1)
    def _():
        block(BLOCK, BLOCK, lambda start, size: w_ref[pl.ds(start, size), :])

    @pl.when(step == steps - 1)
    def _():
        def masked(start, size):
            piece = w_ref[pl.ds(start, size), :last_columns]
            lane = lax.broadcasted_iota(jnp.int32, piece.shape, 1)
            return jnp.where(lane < last, piece, jnp.zeros_like(piece))

        block(last_columns, last, masked)


def head_pass(hidden, head_weight, local_ids, probs, local_targets):
    tokens, depth = hidden.shape
    width = head_weight.shape[1]
    kept = local_ids.shape[1]
    groups = pl.cdiv(width, LANES)
    hi_probs = probs.astype(jnp.bfloat16).astype(jnp.float32)
    lo_probs = probs - hi_probs
    full = lambda shape: pl.BlockSpec(shape, lambda j: (0, 0), pipeline_mode=pl.Buffered(1))
    return pl.pallas_call(
        functools.partial(head_kernel, width),
        grid=(pl.cdiv(width, BLOCK),),
        in_specs=[
            full((tokens, depth)),
            pl.BlockSpec((depth, BLOCK), lambda j: (0, j)),
            full((tokens, kept)),
            full((tokens, kept)),
            full((tokens, kept)),
            full((tokens, 1)),
        ],
        out_specs=[full((2 * tokens, depth)), full((tokens, LANES))],
        out_shape=[
            jax.ShapeDtypeStruct((2 * tokens, depth), jnp.float32),
            jax.ShapeDtypeStruct((tokens, LANES), jnp.float32),
        ],
        scratch_shapes=[pltpu.VMEM((groups, tokens, LANES), jnp.float32)],
        compiler_params=pltpu.CompilerParams(vmem_limit_bytes=58 * 1024 * 1024),
        cost_estimate=pl.CostEstimate(
            flops=6 * tokens * depth * width, bytes_accessed=2 * depth * width,
            transcendentals=2 * tokens * width),
        name="head_pass",
    )(hidden, head_weight, local_ids, hi_probs, lo_probs, local_targets[:, None])


def per_device(hidden, head_weight, teacher_ids, teacher_probs, target_ids):
    width = head_weight.shape[1]
    tokens_local = hidden.shape[0]
    position = lax.axis_index(AXES)
    first_column = position * width
    gather = lambda x: lax.all_gather(x, AXES, axis=0, tiled=True)
    all_hidden = gather(hidden)
    all_ids = gather(jnp.concatenate([teacher_ids, target_ids[:, None]], axis=1))
    all_probs = gather(teacher_probs)
    kept = teacher_ids.shape[1]
    local = all_ids - first_column
    acc, stats = head_pass(all_hidden, head_weight, local[:, :kept], all_probs, local[:, kept])
    tokens = all_hidden.shape[0]
    totals = lax.psum(stats[:, :2], AXES)
    exp_sum, dots = totals[:, 0], totals[:, 1]
    teacher_sum = jnp.sum(all_probs, axis=1)
    scale = LOSS_SCALE * (teacher_sum + CE_WEIGHT) / exp_sum
    part = scale[:, None] * acc[:tokens] - LOSS_SCALE * acc[tokens:]
    summed = lax.psum_scatter(part, AXES, scatter_dimension=0, tiled=True)
    own = lambda x: lax.dynamic_slice_in_dim(x, position * tokens_local, tokens_local)
    own_sum = jnp.sum(teacher_probs, axis=1)
    loss = (
        jnp.sum(teacher_probs * jnp.log(teacher_probs), axis=1)
        - own(dots)
        + (own_sum + CE_WEIGHT) * jnp.log(own(exp_sum))
    )
    return loss, summed.astype(jnp.bfloat16)


def solution(mesh):
    in_specs = (
        P(AXES, None),
        P(None, AXES),
        P(AXES, None),
        P(AXES, None),
        P(AXES),
    )
    out_specs = (P(AXES), P(AXES, None))
    return jax.shard_map(
        per_device, mesh=mesh, in_specs=in_specs, out_specs=out_specs, check_vma=False
    )
```

time: 492 us -> 342 us (0.70)
  other arithmetic: 167 us -> 4.6 us
  local copies, waits for them, and re-layouts: 12.3 us -> 72.5 us
  matrix products: 48.5 us -> 0 us
  Pallas kernels: 0 us -> 41.4 us
  blocking collectives: 260 us -> 219 us
    reduce_sum x5 -> x1, other arithmetic: 167 us -> 0.15 us  [per_device(): jnp.sum(teacher_probs * jnp.log(teacher_probs), axis=1) - own(dots)]
    unnamed x5 -> x6, local copies, waits for them, and re-layouts: 1.07 us -> 69.6 us
    psum x2 -> x1, blocking collectives: 98.8 us -> 36.9 us  [per_device(): totals = lax.psum(stats[:, :2], AXES)]
    dot_general x2 -> x0, matrix products: 48.5 us -> none  [the longest x1 25.1 us: per_device(): jnp.dot(lax.all_gather(hidden, ('dp', 'vocab'), axis=0, tiled=True), head...]
    pallas_call x0 -> x1, Pallas kernels: none -> 41.4 us  [head_pass(): pl.pallas_call(functools.partial(head_kernel, width), grid=(pl.cdiv(width...]
    unnamed x1, blocking collectives: 40.6 us -> 59.4 us
    reshape x1 -> x0, local copies, waits for them, and re-layouts: 5.63 us -> none  [sparse_rows(): return summed.reshape(token_count, columns.shape[0])]
where the time goes in v1:
time: 342 us; the launch traced here: 338 us
  blocking collectives  219 us (64%)
  local copies, waits for them, and re-layouts  72.5 us (21%)
  Pallas kernels  41.4 us (12%)
  other arithmetic  4.6 us (1%)
    all_gather x3, blocking collectives, per_device(): gather = lambda x: lax.all_gather(x, AXES, axis=0, tiled=True)  123 us
    unnamed x6, local copies, waits for them, and re-layouts  69.6 us
    unnamed x1, blocking collectives  59.4 us
    pallas_call x1, Pallas kernels, head_pass(): pl.pallas_call(functools.partial(head_kernel, width), grid=(pl.cdiv(width...  41.4 us
    psum x1, blocking collectives, per_device(): totals = lax.psum(stats[:, :2], AXES)  36.9 us

profile of v1, /device:TPU:1, one launch (start us, length us, event | category | flops | bytes accessed | tf_op | source)
XLA Modules:
  0.0 337.9 jit_solution(15930784626956888205)
XLA Ops:
  0.6 0.7 copy.13
  1.4 0.7 add_bitcast_fusion
  2.1 43.6 %all-gather.1 = s32[32,4,129]{2,1,0:T(4,128)S(1)} all-gather(s32[1,4,129]{2,1,0:T(4,128)S(1)} %add_bitcast_fusion), channel_id=1, replica_groups=mesh['dp'=4,'vocab'=8] {'dp','vocab'}, dimensions={0}, use_global_device_ids=true | all-gather | bytes 68112 | tf_op jit(solution)/shard_map/all_gather | solution.py:132
  45.7 0.6 slice.28.ids_ref
  46.4 0.6 slice.29.targets_ref
  47.0 37.1 %all-gather.2 = f32[32,4,128]{2,1,0:T(4,128)S(1)} all-gather(f32[1,4,128]{2,1,0:T(4,128)} %bitcast.14), channel_id=1, replica_groups=mesh['dp'=4,'vocab'=8] {'dp','vocab'}, dimensions={0}, use_global_device_ids=true | all-gather | bytes 67584 | tf_op jit(solution)/shard_map/all_gather | solution.py:132
  84.1 0.7 fusion
  84.7 0.0 copy-start
  84.7 68.5 %copy.14.w_ref = bf16[3584,8000]{1,0:T(8,128)(2,1)} copy(bf16[3584,8000]{0,1:T(8,128)(2,1)} %param.6) | data formatting | bytes 114688000 | tf_op args[1]
  153.2 0.0 copy-done
  153.2 41.8 %all-gather = bf16[32,4,3584]{2,1,0:T(4,128)(2,1)S(1)} all-gather(bf16[1,4,3584]{2,1,0:T(4,128)(2,1)S(1)} %bitcast.13), channel_id=1, replica_groups=mesh['dp'=4,'vocab'=8] {'dp','vocab'}, dimensions={0}, use_global_device_ids=true | all-gather | bytes 946176 | tf_op jit(solution)/shard_map/all_gather | solution.py:132
  195.0 1.1 reshape.22.hidden_ref
  196.2 41.4 %head_pass.1 = (f32[256,3584]{1,0:T(8,128)}, f32[128,128]{1,0:T(8,128)}) custom-call(bf16[128,3584]{1,0:T(8,128)(2,1)} %reshape.22.hidden_ref, bf16[3584,8000]{1,0:T(8,128)(2,1)} %copy.14.w_ref, s32[128,128]{1,0:T(8,128)} %slice.28.ids_ref, f32[128,128]{1,0:T(8,128)} %get-tuple-element.12.hi_probs_ref, f32[128,128]{1,0:T(8,128)} %get-tuple-element.11.lo_probs_ref, ...), custom_call_target="tpu_custom_call" | custom-call | flops 22020096000 | bytes 57344000 | tf_op jit(solution)/shard_map/head_pass/pallas_call | solution.py:102
  237.5 36.9 %psum.7 = f32[128,2]{1,0:T(8,128)S(1)} all-reduce(f32[128,2]{1,0:T(8,128)} %bitcast.12), channel_id=1, replica_groups=mesh['dp'=4,'vocab'=8] {'dp','vocab'}, use_global_device_ids=true, to_apply=%region_1.0 | all-reduce | flops 256 | bytes 2048 | tf_op jit(solution)/shard_map/psum | solution.py:140
  274.4 0.1 reduce
  274.5 0.1 mul.62
  274.6 0.1 divide_reduce_fusion
  274.7 0.2 log_reduce_fusion
  274.9 0.0 copy-done.1
  274.9 0.2 fusion.1
  275.1 0.5 multiply_add_fusion
  275.6 2.3 multiply_subtract_fusion
  277.9 59.4 %all-reduce.2 = bf16[128,3584]{1,0:T(8,128)(2,1)S(1)} all-reduce(f32[128,3584]{1,0:T(8,128)S(1)} %multiply_subtract_fusion), channel_id=2, replica_groups=mesh['dp'=4,'vocab'=8] {'dp','vocab'}, use_global_device_ids=true, to_apply=%region_4.0.clone | all-reduce | flops 458752 | bytes 2752512
  337.3 0.6 dynamic-slice_convert_fusion
  (4 shorter events, 0.1 us)
Async XLA Ops:
  84.7 68.5 %copy-start = (bf16[4,3584]{1,0:T(4,128)(2,1)S(1)}, bf16[4,3584]{1,0:T(4,128)(2,1)}, u32[]{:S(2)}) copy-start(bf16[4,3584]{1,0:T(4,128)(2,1)} %param.5) | copy-start | bytes 86020
  196.2 78.8 %copy-start.1 = (f32[4,128]{1,0:T(4,128)S(1)}, f32[4,128]{1,0:T(4,128)}, u32[]{:S(2)}) copy-start(f32[4,128]{1,0:T(4,128)} %param.8) | copy-start | bytes 6148

commit v2 on v1

v2 whole, which is shorter than its diff:
```python
import functools
import jax
import jax.numpy as jnp
from jax import lax
from jax.experimental import pallas as pl
from jax.experimental.pallas import tpu as pltpu
from jax.sharding import PartitionSpec as P

SOFT_CAP = 30.0
CE_WEIGHT = 0.5
LOSS_SCALE = 8.0
BLOCK = 512
LANES = 128
ROW_CHUNK = 512
AXES = ("dp", "vocab")
MESH = pl.DeviceIdType.MESH
NT = (((1,), (1,)), ((), ()))


def head_kernel(width, hidden_ref, w_ref, ids_ref, hi_probs_ref, lo_probs_ref, targets_ref,
                acc_ref, stats_ref, sparse_ref):
    step = pl.program_id(0)
    steps = pl.num_programs(0)
    tokens, depth = hidden_ref.shape
    kept = ids_ref.shape[1]
    groups = sparse_ref.shape[0]
    group_rows = 16 * pl.cdiv(groups, 16)

    @pl.when(step == 0)
    def _():
        acc_ref[...] = jnp.zeros_like(acc_ref)
        stats_ref[...] = jnp.zeros_like(stats_ref)
        group_row = lax.broadcasted_iota(jnp.int32, (group_rows, kept), 0)
        lane_row = lax.broadcasted_iota(jnp.int32, (LANES, kept), 0)

        def one_token(t, carry):
            ids = ids_ref[pl.ds(t, 1), :]
            high = jnp.where(group_row == (ids >> 7), 1.0, 0.0).astype(jnp.bfloat16)
            same = lane_row == (ids & 127)
            first = jnp.where(same, hi_probs_ref[pl.ds(t, 1), :], 0.0).astype(jnp.bfloat16)
            second = jnp.where(same, lo_probs_ref[pl.ds(t, 1), :], 0.0).astype(jnp.bfloat16)
            rows = lax.dot_general(
                jnp.concatenate([high, high], axis=1),
                jnp.concatenate([first, second], axis=1),
                NT, preferred_element_type=jnp.float32)
            sparse_ref[:, pl.ds(t, 1), :] = rows[:groups].reshape(groups, 1, LANES)
            return carry

        lax.fori_loop(0, tokens, one_token, 0, unroll=8)

    def block(columns):
        w = w_ref.at[pl.ds(0, columns)]
        logits = lax.dot_general(hidden_ref[...], w[...], NT, preferred_element_type=jnp.float32)
        ratio = jnp.tanh(logits * (1.0 / SOFT_CAP))
        capped = SOFT_CAP * ratio
        slope = 1.0 - ratio * ratio
        lane = lax.broadcasted_iota(jnp.int32, (tokens, columns), 1)
        exps = jnp.exp(capped)
        sparse = jnp.concatenate(
            [sparse_ref[step * (BLOCK // LANES) + i] for i in range(pl.cdiv(columns, LANES))],
            axis=1)[:, :columns]
        sparse = sparse + jnp.where(lane + step * BLOCK == targets_ref[...], CE_WEIGHT, 0.0)
        stats_ref[:, 0:1] += jnp.sum(exps, axis=1, keepdims=True)
        stats_ref[:, 1:2] += jnp.sum(capped * sparse, axis=1, keepdims=True)
        grads = jnp.concatenate([exps * slope, sparse * slope], axis=0).astype(jnp.bfloat16)
        for start in range(0, depth, ROW_CHUNK):
            part = slice(start, start + ROW_CHUNK)
            acc_ref[:, part] += jnp.dot(grads, w[:, part], preferred_element_type=jnp.float32)

    last = width - (pl.cdiv(width, BLOCK) - 1) * BLOCK

    @pl.when(step < steps - 1)
    def _():
        block(BLOCK)

    @pl.when(step == steps - 1)
    def _():
        block(last)


def head_pass(hidden, head_weight, local_ids, probs, local_targets):
    tokens, depth = hidden.shape
    width = head_weight.shape[1]
    kept = local_ids.shape[1]
    groups = pl.cdiv(width, LANES)
    hi_probs = probs.astype(jnp.bfloat16).astype(jnp.float32)
    lo_probs = probs - hi_probs
    full = lambda shape: pl.BlockSpec(shape, lambda j: (0, 0), pipeline_mode=pl.Buffered(1))
    return pl.pallas_call(
        functools.partial(head_kernel, width),
        grid=(pl.cdiv(width, BLOCK),),
        in_specs=[
            full((tokens, depth)),
            pl.BlockSpec((BLOCK, depth), lambda j: (j, 0)),
            full((tokens, kept)),
            full((tokens, kept)),
            full((tokens, kept)),
            full((tokens, 1)),
        ],
        out_specs=[full((2 * tokens, depth)), full((tokens, LANES))],
        out_shape=[
            jax.ShapeDtypeStruct((2 * tokens, depth), jnp.float32),
            jax.ShapeDtypeStruct((tokens, LANES), jnp.float32),
        ],
        scratch_shapes=[pltpu.VMEM((groups, tokens, LANES), jnp.float32)],
        compiler_params=pltpu.CompilerParams(vmem_limit_bytes=58 * 1024 * 1024),
        cost_estimate=pl.CostEstimate(
            flops=6 * tokens * depth * width, bytes_accessed=2 * depth * width,
            transcendentals=2 * tokens * width),
        name="head_pass",
    )(hidden, head_weight.T, local_ids, hi_probs, lo_probs, local_targets[:, None])


def meet(nd, nv):
    d, v = lax.axis_index("dp"), lax.axis_index("vocab")
    barrier = pltpu.get_barrier_semaphore()
    peers_v = [(d, lax.rem(v + o, nv)) for o in range(1, nv)]
    peers_d = [(lax.rem(d + o, nd), v) for o in range(1, nd)]
    for peer in peers_v + peers_d:
        pl.semaphore_signal(barrier, inc=1, device_id=peer, device_id_type=MESH)
    pl.semaphore_wait(barrier, nv + nd - 2)
    return d, v, peers_d, peers_v


def remote(src, dst, send, recv, peer):
    return pltpu.make_async_remote_copy(
        src_ref=src, dst_ref=dst, send_sem=send, recv_sem=recv,
        device_id=peer, device_id_type=MESH)


def gather_kernel(nd, nv, *refs):
    ins, outs = refs[:3], refs[3:6]
    send_v, recv_v, send_d, recv_d = refs[6:]
    d, v, peers_d, peers_v = meet(nd, nv)
    for i in range(3):
        outs[i][d * nv + v] = ins[i][...]
    copies = []
    for o, peer in enumerate(peers_v):
        for i in range(3):
            copy = remote(ins[i], outs[i].at[d * nv + v], send_v.at[i, o], recv_v.at[i, v], peer)
            copy.start()
            copies.append(copy)
    for o, peer in enumerate(peers_v):
        for i in range(3):
            source = peer[1]
            remote(ins[i], outs[i].at[d * nv + source], send_v.at[i, o],
                   recv_v.at[i, source], peer).wait_recv()
    for o, peer in enumerate(peers_d):
        for i in range(3):
            rows = outs[i].at[pl.ds(d * nv, nv)]
            copy = remote(rows, rows, send_d.at[i, o], recv_d.at[i, d], peer)
            copy.start()
            copies.append(copy)
    for o, peer in enumerate(peers_d):
        for i in range(3):
            rows = outs[i].at[pl.ds(peer[0] * nv, nv)]
            remote(rows, rows, send_d.at[i, o], recv_d.at[i, peer[0]], peer).wait_recv()
    for copy in copies:
        copy.wait_send()


def totals_kernel(nd, nv, in_ref, out_ref, slots_v, slots_d, held, send_v, recv_v, send_d, recv_d):
    d, v, peers_d, peers_v = meet(nd, nv)
    copies = []
    for peers, me, src, slots, send, recv, axis, result in (
        (peers_v, v, in_ref, slots_v, send_v, recv_v, 1, held),
        (peers_d, d, held, slots_d, send_d, recv_d, 0, out_ref),
    ):
        for o, peer in enumerate(peers):
            copy = remote(src, slots.at[me], send.at[o], recv.at[me], peer)
            copy.start()
            copies.append(copy)
        slots[me] = src[...]
        for o, peer in enumerate(peers):
            source = peer[axis]
            remote(src, slots.at[source], send.at[o], recv.at[source], peer).wait_recv()
        result[...] = jnp.sum(slots[...], axis=0)
    for copy in copies:
        copy.wait_send()


def reduce_kernel(nd, nv, in_ref, out_ref, slots_d, slots_v, held, send_d, recv_d, send_v, recv_v):
    d, v, peers_d, peers_v = meet(nd, nv)
    copies = []
    for o, peer in enumerate(peers_d):
        copy = remote(in_ref.at[peer[0]], slots_d.at[d], send_d.at[o], recv_d.at[d], peer)
        copy.start()
        copies.append(copy)
    held[...] = in_ref[d].astype(jnp.float32)
    for o, peer in enumerate(peers_d):
        source = peer[0]
        remote(in_ref.at[d], slots_d.at[source], send_d.at[o], recv_d.at[source], peer).wait_recv()
        held[...] += slots_d[source].astype(jnp.float32)
    for o, peer in enumerate(peers_v):
        copy = remote(held.at[peer[1]], slots_v.at[v], send_v.at[o], recv_v.at[v], peer)
        copy.start()
        copies.append(copy)
    total = held[v]
    for o, peer in enumerate(peers_v):
        source = peer[1]
        remote(held.at[v], slots_v.at[source], send_v.at[o], recv_v.at[source], peer).wait_recv()
        total = total + slots_v[source]
    out_ref[...] = total.astype(out_ref.dtype)
    for copy in copies:
        copy.wait_send()


def comm_call(kernel, number, name, args, out_shape, scratch):
    vmem = pl.BlockSpec(memory_space=pltpu.VMEM)
    return pl.pallas_call(
        kernel,
        out_shape=out_shape,
        in_specs=[vmem] * len(args),
        out_specs=[vmem] * len(out_shape),
        scratch_shapes=scratch,
        compiler_params=pltpu.CompilerParams(
            collective_id=number, has_side_effects=True, vmem_limit_bytes=48 * 1024 * 1024),
        name=name,
    )(*args)


def per_device(nd, nv, hidden, head_weight, teacher_ids, teacher_probs, target_ids):
    width = head_weight.shape[1]
    local_tokens, kept = teacher_ids.shape
    depth = hidden.shape[1]
    count = nd * nv
    tokens = count * local_tokens
    position = lax.axis_index(AXES)
    sems = lambda *shape: pltpu.SemaphoreType.DMA(shape)
    rows = local_tokens * depth // LANES
    pad = 8 * pl.cdiv(local_tokens + 1, 8)
    target_row = jnp.pad(target_ids, (0, kept - local_tokens))[None, :]
    ids = jnp.pad(jnp.concatenate([teacher_ids, target_row], axis=0),
                  ((0, pad - local_tokens - 1), (0, 0)))
    probs = jnp.pad(teacher_probs, ((0, pad - local_tokens), (0, 0)))
    args = (hidden.reshape(rows, LANES), ids, probs)
    got = comm_call(
        functools.partial(gather_kernel, nd, nv), 0, "gather_inputs", args,
        [jax.ShapeDtypeStruct((count,) + a.shape, a.dtype) for a in args],
        [sems(3, nv), sems(3, nv), sems(3, nd), sems(3, nd)])
    all_hidden = got[0].reshape(tokens, depth)
    local = got[1] - position * width
    local_ids = local[:, :local_tokens].reshape(tokens, kept)
    local_targets = local[:, local_tokens, :local_tokens].reshape(tokens)
    all_probs = got[2][:, :local_tokens].reshape(tokens, kept)
    acc, stats = head_pass(all_hidden, head_weight, local_ids, all_probs, local_targets)
    block = (8, tokens)
    totals = comm_call(
        functools.partial(totals_kernel, nd, nv), 1, "sum_stats", (stats[:, :8].T,),
        [jax.ShapeDtypeStruct(block, jnp.float32)],
        [pltpu.VMEM((nv,) + block, jnp.float32), pltpu.VMEM((nd,) + block, jnp.float32),
         pltpu.VMEM(block, jnp.float32), sems(nv), sems(nv), sems(nd), sems(nd)])[0]
    exp_sum, dots = totals[0], totals[1]
    teacher_sum = jnp.sum(all_probs, axis=1)
    scale = LOSS_SCALE * (teacher_sum + CE_WEIGHT) / exp_sum
    part = (scale[:, None] * acc[:tokens] - LOSS_SCALE * acc[tokens:]).astype(jnp.bfloat16)
    piece = (rows, LANES)
    grad = comm_call(
        functools.partial(reduce_kernel, nd, nv), 2, "sum_grads",
        (part.reshape((nd, nv) + piece),),
        [jax.ShapeDtypeStruct(piece, jnp.bfloat16)],
        [pltpu.VMEM((nd, nv) + piece, jnp.bfloat16), pltpu.VMEM((nv,) + piece, jnp.float32),
         pltpu.VMEM((nv,) + piece, jnp.float32), sems(nd), sems(nd), sems(nv), sems(nv)])[0]
    own = lambda x: lax.dynamic_slice_in_dim(x, position * local_tokens, local_tokens)
    own_sum = jnp.sum(teacher_probs, axis=1)
    loss = (
        jnp.sum(teacher_probs * jnp.log(teacher_probs), axis=1)
        - own(dots)
        + (own_sum + CE_WEIGHT) * jnp.log(own(exp_sum))
    )
    return loss, grad.reshape(local_tokens, depth)


def solution(mesh):
    in_specs = (
        P(AXES, None),
        P(None, AXES),
        P(AXES, None),
        P(AXES, None),
        P(AXES),
    )
    out_specs = (P(AXES), P(AXES, None))
    return jax.shard_map(
        functools.partial(per_device, mesh.shape["dp"], mesh.shape["vocab"]),
        mesh=mesh, in_specs=in_specs, out_specs=out_specs, check_vma=False
    )
```

time: 342 us -> 127 us (0.37)
  blocking collectives: 219 us -> 0 us
  Pallas kernels: 41.4 us -> 112 us
  local copies, waits for them, and re-layouts: 72.5 us -> 8.24 us
    all_gather x3 -> x0, blocking collectives: 123 us -> none  [per_device(): gather = lambda x: lax.all_gather(x, AXES, axis=0, tiled=True)]
    unnamed x6 -> x0, local copies, waits for them, and re-layouts: 69.6 us -> none
    pallas_call x0 -> x3, Pallas kernels: none -> 61.6 us  [comm_call(): pl.pallas_call(kernel, out_shape=out_shape, in_specs=[vmem] * len(args),...]
    unnamed x1 -> x0, blocking collectives: 59.4 us -> none
    psum x1 -> x0, blocking collectives: 36.9 us -> none  [per_device(): totals = lax.psum(stats[:, :2], AXES)]
    pallas_call x1, Pallas kernels: 41.4 us -> 50.4 us  [head_pass(): pl.pallas_call(functools.partial(head_kernel, width), grid=(pl.cdiv(width...]
    reshape x0 -> x4, local copies, waits for them, and re-layouts: none -> 4.48 us  [the longest x1 1.95 us: per_device(): all_hidden = got[0].reshape(tokens, depth)]
where the time goes in v2:
time: 127 us; the launch traced here: 126 us
  Pallas kernels  112 us (88%)
  local copies, waits for them, and re-layouts  8.24 us (6%)
  other arithmetic  5.27 us (4%)
    pallas_call x3, Pallas kernels, comm_call(): pl.pallas_call(kernel, out_shape=out_shape, in_specs=[vmem] * len(args),...  61.6 us
    pallas_call x1, Pallas kernels, head_pass(): pl.pallas_call(functools.partial(head_kernel, width), grid=(pl.cdiv(width...  50.4 us

profile of v2, /device:TPU:1, one launch (start us, length us, event | category | flops | bytes accessed | tf_op | source)
XLA Modules:
  0.0 126.3 jit_solution(14673421371021406088)
XLA Ops:
  0.6 0.7 pad_bitcast_fusion
  1.3 0.8 fusion.3
  2.1 0.7 pad_add_fusion
  2.8 0.7 pad.14.refs_2_
  3.5 0.8 reshape.42.refs_0_
  4.3 26.6 %gather_inputs.1 = (bf16[32,112,128]{2,1,0:T(8,128)(2,1)S(1)}, s32[32,8,128]{2,1,0:T(8,128)S(1)}, f32[32,8,128]{2,1,0:T(8,128)S(1)}) custom-call(bf16[112,128]{1,0:T(8,128)(2,1)S(1)} %reshape.42.refs_0_, s32[8,128]{1,0:T(8,128)S(1)} %pad.13.refs_1_, f32[8,128]{1,0:T(8,128)S(1)} %pad.14.refs_2_), custom_call_target="tpu_custom_call" | custom-call | tf_op jit(solution)/shard_map/gather_inputs/pallas_call | solution.py:210
  30.8 1.9 %reshape.43.hidden_ref = bf16[128,3584]{1,0:T(8,128)(2,1)} reshape(bf16[32,112,128]{2,1,0:T(8,128)(2,1)S(1)} %get-tuple-element.7) | data formatting | bytes 1835008 | tf_op jit(solution)/shard_map/reshape | solution.py:241
  32.8 0.1 slice_reduce_fusion.1
  32.9 0.1 mul.50
  33.0 0.7 fusion
  33.7 0.1 slice_reduce_fusion
  33.8 0.6 slice.32
  34.4 0.7 broadcast_in_dim_reshape_squeeze.4.targets_ref
  35.1 50.4 %head_pass.1 = (f32[256,3584]{1,0:T(8,128)}, f32[128,128]{1,0:T(8,128)}) custom-call(bf16[128,3584]{1,0:T(8,128)(2,1)} %reshape.43.hidden_ref, bf16[8000,3584]{1,0:T(8,128)(2,1)} %bitcast.19, s32[128,128]{1,0:T(8,128)} %bitcast.18, f32[128,128]{1,0:T(8,128)} %get-tuple-element.17.hi_probs_ref, f32[128,128]{1,0:T(8,128)} %get-tuple-element.16.lo_probs_ref, ...), custom_call_target="tpu_custom_call" | custom-call | flops 22020096000 | bytes 57344000 | tf_op jit(solution)/shard_map/head_pass/pallas_call | solution.py:89
  85.5 0.9 copy.10
  86.5 9.7 %sum_stats.1 = f32[8,128]{1,0:T(8,128)S(1)} custom-call(f32[8,128]{1,0:T(8,128)S(1)} %slice_bitcast_fusion.in_ref), custom_call_target="tpu_custom_call" | custom-call | tf_op jit(solution)/shard_map/sum_stats/pallas_call | solution.py:210
  96.2 2.4 %subtract_convert_fusion = bf16[128,3584]{1,0:T(8,128)(2,1)S(1)} fusion(f32[256,3584]{1,0:T(8,128)} %get-tuple-element.11, f32[128]{0:T(128)S(1)} %bitcast_divide_fusion), kind=kLoop, calls=%fused_computation | loop fusion | flops 1835008 | bytes 4588032 | tf_op jit(solution)/shard_map/convert_element_type | solution.py:256
  98.6 0.6 fusion.2
  99.2 1.1 reshape.46.in_ref
  100.3 25.4 %sum_grads.1 = bf16[112,128]{1,0:T(8,128)(2,1)S(1)} custom-call(bf16[4,8,112,128]{3,2,1,0:T(8,128)(2,1)S(1)} %reshape.46.in_ref), custom_call_target="tpu_custom_call" | custom-call | tf_op jit(solution)/shard_map/sum_grads/pallas_call | solution.py:210
  125.7 0.6 reshape.47
  (6 shorter events, 0.0 us)

commit v3 on v2

--- a/solution.py
+++ b/solution.py
@@ -21,7 +21,7 @@
                 acc_ref, stats_ref, sparse_ref):
     step = pl.program_id(0)
     steps = pl.num_programs(0)
-    tokens, depth = hidden_ref.shape
+    depth, tokens = hidden_ref.shape
     kept = ids_ref.shape[1]
     groups = sparse_ref.shape[0]
     group_rows = 16 * pl.cdiv(groups, 16)
@@ -50,7 +50,7 @@
 
     def block(columns):
         w = w_ref.at[pl.ds(0, columns)]
-        logits = lax.dot_general(hidden_ref[...], w[...], NT, preferred_element_type=jnp.float32)
+        logits = jnp.dot(w[...], hidden_ref[...], preferred_element_type=jnp.float32).T
         ratio = jnp.tanh(logits * (1.0 / SOFT_CAP))
         capped = SOFT_CAP * ratio
         slope = 1.0 - ratio * ratio
@@ -90,7 +90,7 @@
         functools.partial(head_kernel, width),
         grid=(pl.cdiv(width, BLOCK),),
         in_specs=[
-            full((tokens, depth)),
+            full((depth, tokens)),
             pl.BlockSpec((BLOCK, depth), lambda j: (j, 0)),
             full((tokens, kept)),
             full((tokens, kept)),
@@ -108,7 +108,7 @@
             flops=6 * tokens * depth * width, bytes_accessed=2 * depth * width,
             transcendentals=2 * tokens * width),
         name="head_pass",
-    )(hidden, head_weight.T, local_ids, hi_probs, lo_probs, local_targets[:, None])
+    )(hidden.T, head_weight.T, local_ids, hi_probs, lo_probs, local_targets[:, None])
 
 
 def meet(nd, nv):

time: 127 us -> 152 us (1.20)
  Pallas kernels: 112 us -> 137 us
    pallas_call x1, Pallas kernels: 50.4 us -> 75.2 us  [head_pass(): pl.pallas_call(functools.partial(head_kernel, width), grid=(pl.cdiv(width...]
where the time goes in v3:
time: 152 us; the launch traced here: 151 us
  Pallas kernels  137 us (90%)
  local copies, waits for them, and re-layouts  8.57 us (6%)
  other arithmetic  5.27 us (3%)
    pallas_call x1, Pallas kernels, head_pass(): pl.pallas_call(functools.partial(head_kernel, width), grid=(pl.cdiv(width...  75.2 us
    pallas_call x3, Pallas kernels, comm_call(): pl.pallas_call(kernel, out_shape=out_shape, in_specs=[vmem] * len(args),...  61.6 us

profile of v3, /device:TPU:1, one launch (start us, length us, event | category | flops | bytes accessed | tf_op | source)
XLA Modules:
  0.0 151.4 jit_solution(5733817398024026863)
XLA Ops:
  0.6 0.7 pad_bitcast_fusion
  1.3 0.8 fusion.3
  2.1 0.7 pad_add_fusion
  2.8 0.7 pad.14.refs_2_
  3.5 0.8 reshape.42.refs_0_
  4.3 26.6 %gather_inputs.1 = (bf16[32,112,128]{2,1,0:T(8,128)(2,1)S(1)}, s32[32,8,128]{2,1,0:T(8,128)S(1)}, f32[32,8,128]{2,1,0:T(8,128)S(1)}) custom-call(bf16[112,128]{1,0:T(8,128)(2,1)S(1)} %reshape.42.refs_0_, s32[8,128]{1,0:T(8,128)S(1)} %pad.13.refs_1_, f32[8,128]{1,0:T(8,128)S(1)} %pad.14.refs_2_), custom_call_target="tpu_custom_call" | custom-call | tf_op jit(solution)/shard_map/gather_inputs/pallas_call | solution.py:210
  30.8 1.0 reshape.43
  31.9 1.3 copy.9
  33.1 0.1 slice_reduce_fusion.1
  33.3 0.1 mul.50
  33.4 0.7 fusion
  34.1 0.1 slice_reduce_fusion
  34.1 0.6 slice.32
  34.7 0.7 broadcast_in_dim_reshape_squeeze.4.targets_ref
  35.4 75.2 %head_pass.1 = (f32[256,3584]{1,0:T(8,128)}, f32[128,128]{1,0:T(8,128)}) custom-call(bf16[3584,128]{1,0:T(8,128)(2,1)} %bitcast.18, bf16[8000,3584]{1,0:T(8,128)(2,1)} %bitcast.21, s32[128,128]{1,0:T(8,128)} %bitcast.20, f32[128,128]{1,0:T(8,128)} %get-tuple-element.17.hi_probs_ref, f32[128,128]{1,0:T(8,128)} %get-tuple-element.16.lo_probs_ref, ...), custom_call_target="tpu_custom_call" | custom-call | flops 22020096000 | bytes 57344000 | tf_op jit(solution)/shard_map/head_pass/pallas_call | solution.py:89
  110.7 0.9 copy.11
  111.6 9.7 %sum_stats.1 = f32[8,128]{1,0:T(8,128)S(1)} custom-call(f32[8,128]{1,0:T(8,128)S(1)} %slice_bitcast_fusion.in_ref), custom_call_target="tpu_custom_call" | custom-call | tf_op jit(solution)/shard_map/sum_stats/pallas_call | solution.py:210
  121.4 2.4 %subtract_convert_fusion = bf16[128,3584]{1,0:T(8,128)(2,1)S(1)} fusion(f32[256,3584]{1,0:T(8,128)} %get-tuple-element.11, f32[128]{0:T(128)S(1)} %bitcast_divide_fusion), kind=kLoop, calls=%fused_computation | loop fusion | flops 1835008 | bytes 4588032 | tf_op jit(solution)/shard_map/convert_element_type | solution.py:256
  123.7 0.6 fusion.2
  124.3 1.1 reshape.46.in_ref
  125.5 25.4 %sum_grads.1 = bf16[112,128]{1,0:T(8,128)(2,1)S(1)} custom-call(bf16[4,8,112,128]{3,2,1,0:T(8,128)(2,1)S(1)} %reshape.46.in_ref), custom_call_target="tpu_custom_call" | custom-call | tf_op jit(solution)/shard_map/sum_grads/pallas_call | solution.py:210
  150.8 0.6 reshape.47
  (6 shorter events, 0.0 us)

commit v4 on v2

--- a/solution.py
+++ b/solution.py
@@ -9,7 +9,7 @@
 SOFT_CAP = 30.0
 CE_WEIGHT = 0.5
 LOSS_SCALE = 8.0
-BLOCK = 512
+BLOCK = 1024
 LANES = 128
 ROW_CHUNK = 512
 AXES = ("dp", "vocab")

time: 127 us -> 123 us (0.969)
  Pallas kernels: 112 us -> 109 us
    pallas_call x1, Pallas kernels: 50.4 us -> 47.1 us  [head_pass(): pl.pallas_call(functools.partial(head_kernel, width), grid=(pl.cdiv(width...]
where the time goes in v4:
time: 123 us
  Pallas kernels  109 us (89%)
  local copies, waits for them, and re-layouts  8.24 us (7%)
  other arithmetic  5.27 us (4%)
    pallas_call x3, Pallas kernels, comm_call(): pl.pallas_call(kernel, out_shape=out_shape, in_specs=[vmem] * len(args),...  61.6 us
    pallas_call x1, Pallas kernels, head_pass(): pl.pallas_call(functools.partial(head_kernel, width), grid=(pl.cdiv(width...  47.1 us

profile of v4, /device:TPU:1, one launch (start us, length us, event | category | flops | bytes accessed | tf_op | source)
XLA Modules:
  0.0 123.0 jit_solution(7913495770868065056)
XLA Ops:
  0.6 0.7 pad_bitcast_fusion
  1.3 0.8 fusion.3
  2.1 0.7 pad_add_fusion
  2.8 0.7 pad.14.refs_2_
  3.5 0.8 reshape.42.refs_0_
  4.3 26.6 %gather_inputs.1 = (bf16[32,112,128]{2,1,0:T(8,128)(2,1)S(1)}, s32[32,8,128]{2,1,0:T(8,128)S(1)}, f32[32,8,128]{2,1,0:T(8,128)S(1)}) custom-call(bf16[112,128]{1,0:T(8,128)(2,1)S(1)} %reshape.42.refs_0_, s32[8,128]{1,0:T(8,128)S(1)} %pad.13.refs_1_, f32[8,128]{1,0:T(8,128)S(1)} %pad.14.refs_2_), custom_call_target="tpu_custom_call" | custom-call | tf_op jit(solution)/shard_map/gather_inputs/pallas_call | solution.py:210
  30.8 1.9 %reshape.43.hidden_ref = bf16[128,3584]{1,0:T(8,128)(2,1)} reshape(bf16[32,112,128]{2,1,0:T(8,128)(2,1)S(1)} %get-tuple-element.7) | data formatting | bytes 1835008 | tf_op jit(solution)/shard_map/reshape | solution.py:241
  32.8 0.1 slice_reduce_fusion.1
  32.9 0.1 mul.50
  33.0 0.7 fusion
  33.7 0.1 slice_reduce_fusion
  33.8 0.6 slice.32
  34.4 0.7 broadcast_in_dim_reshape_squeeze.4.targets_ref
  35.1 47.1 %head_pass.1 = (f32[256,3584]{1,0:T(8,128)}, f32[128,128]{1,0:T(8,128)}) custom-call(bf16[128,3584]{1,0:T(8,128)(2,1)} %reshape.43.hidden_ref, bf16[8000,3584]{1,0:T(8,128)(2,1)} %bitcast.19, s32[128,128]{1,0:T(8,128)} %bitcast.18, f32[128,128]{1,0:T(8,128)} %get-tuple-element.17.hi_probs_ref, f32[128,128]{1,0:T(8,128)} %get-tuple-element.16.lo_probs_ref, ...), custom_call_target="tpu_custom_call" | custom-call | flops 22020096000 | bytes 57344000 | tf_op jit(solution)/shard_map/head_pass/pallas_call | solution.py:89
  82.2 0.9 copy.10
  83.2 9.7 %sum_stats.1 = f32[8,128]{1,0:T(8,128)S(1)} custom-call(f32[8,128]{1,0:T(8,128)S(1)} %slice_bitcast_fusion.in_ref), custom_call_target="tpu_custom_call" | custom-call | tf_op jit(solution)/shard_map/sum_stats/pallas_call | solution.py:210
  92.9 2.4 %subtract_convert_fusion = bf16[128,3584]{1,0:T(8,128)(2,1)S(1)} fusion(f32[256,3584]{1,0:T(8,128)} %get-tuple-element.11, f32[128]{0:T(128)S(1)} %bitcast_divide_fusion), kind=kLoop, calls=%fused_computation | loop fusion | flops 1835008 | bytes 4588032 | tf_op jit(solution)/shard_map/convert_element_type | solution.py:256
  95.3 0.6 fusion.2
  95.9 1.1 reshape.46.in_ref
  97.0 25.4 %sum_grads.1 = bf16[112,128]{1,0:T(8,128)(2,1)S(1)} custom-call(bf16[4,8,112,128]{3,2,1,0:T(8,128)(2,1)S(1)} %reshape.46.in_ref), custom_call_target="tpu_custom_call" | custom-call | tf_op jit(solution)/shard_map/sum_grads/pallas_call | solution.py:210
  122.4 0.6 reshape.47
  (6 shorter events, 0.0 us)
